TPU v7x, 32 devices: a whole 2x2x4 slice. The times are simulated.
32 devices in a mesh: line: 16 (over z, y, x), tile: 2 (over core).
Axes of the slice: x: 2, y: 2, z: 4, core: 2. Of those that a mesh axis runs over, the one named last changes fastest.
Arguments:
- traces: bfloat16 [8192, 2048], P(('line', 'tile')), may hold values from -6 to 6
- trace_line: int32 [8192], P(('line', 'tile')), may hold values from 0 to 15, as said below
- trace_bin: int32 [8192], P(('line', 'tile')), may hold values from 0 to 127, as said below
- block_offset: int32 [64], P(('line', 'tile')), may hold values from 0 to 3
- nmo_coef: bfloat16 [16, 4, 8, 2048], P('line'), may hold values from -4 to 4
- band_shift: int32 [16, 4, 2048], P('line'), may hold values from 0 to 120
- bandpass: float32 [31, 2048], replicated, may hold values from -1 to 1
- fold: int32 [16, 128], P('line', 'tile'), may hold values from 4 to 20
Outputs:
- stack: float32 [16, 128, 2048], P('line', 'tile')
Inputs may be any that keep to these rules, and one draw needn't show every extreme that they name: `trace_line`: of one reader device's 256 traces at most 32 go to one line, and in every draw each device sends exactly 32 to some line. `trace_bin`: the bins of a line form 2 tiles of 64 consecutive bins; of one reader device's traces at most 16 go to one tile of one line, and in every draw each device sends exactly 16 to some tile of some line.
All inputs are finite; a program needn't handle non-finite values.
Results may differ from a plain program's by a relative error of at most 0.0003.
Values may be sent and summed in bfloat16 or wider, within the bound.
A program may use at most 64 MiB of HBM per device.

v0:
```python
import jax
import jax.numpy as jnp
from jax import lax
from jax.sharding import PartitionSpec as P


def windows(data, left):
    rows_count = data.shape[0]
    length = data.shape[1]
    groups = length // 128
    padded = jnp.concatenate(
        [
            jnp.zeros((rows_count, left), data.dtype),
            data,
            jnp.zeros((rows_count, 256 - left), data.dtype),
        ],
        1,
    )
    first = padded[:, :length].reshape(rows_count, groups, 128)
    second = padded[:, 128 : length + 128].reshape(rows_count, groups, 128)
    return jnp.concatenate([first, second], 2)


def moveout_matrix(coef_rows, shift_rows):
    taps_count = coef_rows.shape[0]
    groups = coef_rows.shape[1] // 128
    column = jnp.arange(128, dtype=jnp.int32).reshape(1, 1, 128)
    position = jnp.arange(256, dtype=jnp.int32).reshape(1, 256, 1)
    shifts = shift_rows.reshape(groups, 1, 128)
    weights = coef_rows.astype(jnp.float32).reshape(taps_count, groups, 1, 128)
    matrix = jnp.zeros((groups, 256, 128), jnp.float32)
    for tap_index in range(taps_count):
        matrix = matrix + jnp.where(
            position == column + shifts + tap_index, weights[tap_index], 0.0
        )
    return matrix.astype(jnp.bfloat16)


def bandpass_matrix(taps):
    taps_count = taps.shape[0]
    groups = taps.shape[1] // 128
    half = (taps_count - 1) // 2
    column = jnp.arange(128, dtype=jnp.int32).reshape(1, 1, 128)
    position = jnp.arange(256, dtype=jnp.int32).reshape(1, 256, 1)
    weights = taps.reshape(taps_count, groups, 1, 128)
    matrix = jnp.zeros((groups, 256, 128), jnp.float32)
    for tap_index in range(taps_count):
        matrix = matrix + jnp.where(
            position == column + 64 + tap_index - half, weights[tap_index], 0.0
        )
    return matrix


def apply_filter(stacked, matrix):
    rows_count = stacked.shape[0]
    result = jnp.einsum(
        "rgw,gwc->rgc",
        windows(stacked, 64),
        matrix,
        precision=lax.Precision.HIGHEST,
        preferred_element_type=jnp.float32,
    )
    return result.reshape(rows_count, -1)


def moveout(received, received_meta, nmo_coef, band_shift, bins_total):
    slot_count, length = received.shape
    window_rows = windows(received, 0)
    slot_class = jnp.where(received_meta >= 0, received_meta // bins_total, -1)
    corrected = jnp.zeros((slot_count, length // 128, 128), jnp.float32)
    for offset_index in range(nmo_coef.shape[1]):
        matrix = moveout_matrix(nmo_coef[0, offset_index], band_shift[0, offset_index])
        product = jnp.einsum(
            "sgw,gwc->sgc", window_rows, matrix, preferred_element_type=jnp.float32
        )
        corrected = corrected + jnp.where((slot_class == offset_index)[:, None, None], product, 0.0)
    return corrected.reshape(slot_count, length)


def ranks(keys, key_count):
    onehot = (keys[:, None] == jnp.arange(key_count, dtype=jnp.int32)[None, :]).astype(jnp.int32)
    running = jnp.cumsum(onehot, 0)
    return jnp.sum(onehot * running, 1) - 1


def slot_sources(slot_of_trace, total_slots, traces, meta_values):
    trace_iota = jnp.arange(traces.shape[0], dtype=jnp.int32)
    match = jnp.arange(total_slots, dtype=jnp.int32)[:, None] == slot_of_trace[None, :]
    source = jnp.sum(jnp.where(match, trace_iota[None, :], 0), 1)
    filled = jnp.any(match, 1)
    rows_out = jnp.where(
        filled[:, None], jnp.take(traces, source, axis=0), jnp.zeros((), traces.dtype)
    )
    meta_out = jnp.where(filled, jnp.take(meta_values, source, axis=0), -1)
    return (rows_out, meta_out)


def body(traces, trace_line, trace_bin, block_offset, nmo_coef, band_shift, bandpass, fold):
    line_count = lax.axis_size("line")
    tile_count = lax.axis_size("tile")
    trace_count, length = traces.shape
    block_rows = trace_count // block_offset.shape[0]
    bin_share = fold.shape[1]
    bins_total = bin_share * tile_count
    capacity = 2 * trace_count // line_count
    trace_class = jnp.repeat(block_offset, block_rows)
    meta_values = trace_class * bins_total + trace_bin
    filter_weights = bandpass_matrix(bandpass)
    fold_share = fold[0].astype(jnp.float32)[:, None]
    slot_of_trace = trace_line * capacity + ranks(trace_line, line_count)
    rows_out, meta_out = slot_sources(slot_of_trace, line_count * capacity, traces, meta_values)
    received, received_meta = (
        lax.all_to_all(
            rows_out.reshape(line_count, capacity, length),
            "line",
            split_axis=0,
            concat_axis=0,
            tiled=True,
        ),
        lax.all_to_all(
            meta_out.reshape(line_count, capacity), "line", split_axis=0, concat_axis=0, tiled=True
        ),
    )
    flat_meta = received_meta.reshape(-1)
    corrected = moveout(received.reshape(-1, length), flat_meta, nmo_coef, band_shift, bins_total)
    bin_ids = jnp.where(flat_meta >= 0, flat_meta % bins_total, -1)
    selector = (jnp.arange(bins_total, dtype=jnp.int32)[:, None] == bin_ids[None, :]).astype(
        jnp.float32
    )
    stacked = jnp.dot(
        selector, corrected, precision=lax.Precision.HIGHEST, preferred_element_type=jnp.float32
    )
    summed = lax.psum_scatter(
        apply_filter(stacked, filter_weights), "tile", scatter_dimension=0, tiled=True
    )
    return (summed / fold_share)[None]


def solution(mesh):
    placed = (
        P(("line", "tile"), None),
        P(("line", "tile")),
        P(("line", "tile")),
        P(("line", "tile")),
        P("line", None, None, None),
        P("line", None, None),
        P(),
        P("line", "tile"),
    )
    return jax.shard_map(
        body, mesh=mesh, in_specs=placed, out_specs=P("line", "tile", None), check_vma=False
    )
```

profile of v0, /device:TPU:0, one launch (start us, length us, event | category | flops | bytes accessed | tf_op | source)
XLA Modules:
  0.0 171.7 jit_solution(18412641605186944365)
XLA Ops:
  6.5 0.8 fusion.206
  8.1 0.8 fusion.205
  10.6 0.7 bitcast_add_fusion
  11.4 3.5 %gather_fusion = s32[512]{0:T(512)S(1)} fusion(s32[256]{0:T(256)S(1)} %bitcast_add_fusion, s32[1024]{0:T(1024)S(1)} %pad_clamp_fusion), kind=kCustom, calls=%fused_computation | custom fusion | bytes 6144 | tf_op jit(solution)/shard_map/jit(_take)/gather | solution.py:94
  15.7 8.3 %all-to-all-start = ((s32[16,1,32]{2,1,0:T(1,128)}), s32[16,1,32]{2,1,0:T(1,128)S(1)}, u32[]{:S(2)}, u32[]{:S(2)}) async-start(s32[16,1,32]{2,1,0:T(1,128)} %bitcast.36), calls=%async_computation | async-start | bytes 16384 | tf_op jit(solution)/shard_map/all_to_all | solution.py:120
  24.5 2.5 %gather_fusion.1 = bf16[512,2048]{1,0:T(8,128)(2,1)S(1)} fusion(bf16[256,2048]{1,0:T(8,128)(2,1)S(1)} %copy-done, s32[1024]{0:T(1024)S(1)} %pad_clamp_fusion), kind=kCustom, calls=%fused_computation.1 | custom fusion | bytes 4196352 | tf_op jit(solution)/shard_map/jit(_take)/gather | solution.py:92
  27.6 0.7 iota_compare_fusion.35
  28.3 0.7 iota_compare_fusion.37
  29.8 0.7 iota_compare_fusion.41
  34.9 0.7 iota_compare_fusion.55
  35.6 0.7 iota_compare_fusion.57
  36.3 0.7 iota_compare_fusion.59
  38.5 1.6 select_select_fusion
  40.7 7.0 %all-to-all-start.1 = ((bf16[16,32,2048]{2,1,0:T(8,128)(2,1)}), bf16[16,32,2048]{2,1,0:T(8,128)(2,1)S(1)}, u32[]{:S(2)}, u32[]{:S(2)}) async-start(bf16[16,32,2048]{2,1,0:T(8,128)(2,1)} %select_select_fusion), calls=%async_computation.1 | async-start | bytes 4194304 | tf_op jit(solution)/shard_map/all_to_all | solution.py:113
  48.0 1.3 iota_compare_fusion.65
  49.3 1.3 iota_add_fusion.3
  50.6 1.3 iota_add_fusion.2
  51.9 1.3 iota_add_fusion.1
  58.0 32.5 %all-to-all-done.1 = bf16[16,32,2048]{2,1,0:T(8,128)(2,1)S(1)} async-done(((bf16[16,32,2048]{2,1,0:T(8,128)(2,1)}), bf16[16,32,2048]{2,1,0:T(8,128)(2,1)S(1)}, u32[]{:S(2)}, u32[]{:S(2)}) %all-to-all-start.1) | async-done | bytes 2097184 | tf_op jit(solution)/shard_map/all_to_all | solution.py:113
  90.5 1.5 pad_slice_fusion
  92.0 3.9 %copy.36 = bf16[512,2048]{0,1:T(8,128)(2,1)} copy(bf16[512,2048]{1,0:T(8,128)(2,1)} %pad_slice_fusion) | data formatting | bytes 4194304 | tf_op jit(solution)/shard_map/slice | solution.py:20
  95.9 3.9 %copy.38 = bf16[512,16,128]{2,0,1:T(8,128)(2,1)} copy(bf16[512,16,128]{0,2,1:T(8,128)(2,1)} %bitcast.118) | data formatting | bytes 4194304 | tf_op jit(solution)/shard_map/reshape | solution.py:20
  101.1 1.0 copy-done.1
  102.2 7.4 %fusion.65 = f32[16,128,512]{2,1,0:T(8,128)S(1)} fusion(f32[16,128]{1,0:T(8,128)S(1)} %bitcast.183, s32[16,128]{1,0:T(8,128)S(1)} %copy-done.76, f32[16,128]{1,0:T(8,128)S(1)} %bitcast.182, s32[16,128]{1,0:T(8,128)S(1)} %copy-done.75, f32[16,128]{1,0:T(8,128)S(1)} %bitcast.181, s32[16,128]{1,0:T(8,128)S(1)} %copy-done.74, f32[16,128]{1,0:T(8,128)S(1)} %bitcast.180, ...), kind=kOutput, calls=%fused_computation.109 | convolution fusion | flops 557842432 | bytes 8519680 | tf_op jit(solution)/shard_map/sgw,gwc->sgc/dot_general | solution.py:73
  109.8 7.4 %fusion.66 = f32[16,128,512]{2,1,0:T(8,128)S(1)} fusion(f32[16,128]{1,0:T(8,128)S(1)} %bitcast.186, s32[16,128]{1,0:T(8,128)S(1)} %copy-done.68, f32[16,128]{1,0:T(8,128)S(1)} %bitcast.187, s32[16,128]{1,0:T(8,128)S(1)} %copy-done.67, f32[16,128]{1,0:T(8,128)S(1)} %bitcast.188, s32[16,128]{1,0:T(8,128)S(1)} %copy-done.66, f32[16,128]{1,0:T(8,128)S(1)} %bitcast.189, ...), kind=kOutput, calls=%fused_computation.110 | convolution fusion | flops 557842432 | bytes 8519680 | tf_op jit(solution)/shard_map/sgw,gwc->sgc/dot_general | solution.py:73
  117.5 7.4 %fusion.67 = f32[16,128,512]{2,1,0:T(8,128)S(1)} fusion(f32[16,128]{1,0:T(8,128)S(1)} %bitcast.175, s32[16,128]{1,0:T(8,128)S(1)} %copy-done.60, f32[16,128]{1,0:T(8,128)S(1)} %bitcast.174, s32[16,128]{1,0:T(8,128)S(1)} %copy-done.59, f32[16,128]{1,0:T(8,128)S(1)} %bitcast.173, s32[16,128]{1,0:T(8,128)S(1)} %copy-done.58, f32[16,128]{1,0:T(8,128)S(1)} %bitcast.172, ...), kind=kOutput, calls=%fused_computation.111 | convolution fusion | flops 557842432 | bytes 8519680 | tf_op jit(solution)/shard_map/sgw,gwc->sgc/dot_general | solution.py:73
  125.0 4.7 %select_add_fusion = f32[16,128,512]{2,1,0:T(8,128)S(1)} fusion(f32[16,128,512]{2,1,0:T(8,128)S(1)} %fusion.67, f32[16,128,512]{2,1,0:T(8,128)S(1)} %fusion.66, f32[16,128,512]{2,1,0:T(8,128)S(1)} %fusion.65, pred[512]{0:T(512)(128)(4,1)S(1)} %copy-done.80, pred[512]{0:T(512)(128)(4,1)S(1)} %copy-done.79, pred[512]{0:T(512)(128)(4,1)S(1)} %copy-done.78, ...), kind=kOutput, calls=%fused_computation.3 | convolution fusion | flops 565182464 | bytes 21104640 | tf_op jit(solution)/shard_map/sgw,gwc->sgc/dot_general | solution.py:73
  129.7 2.5 %fusion.202 = f32[128,2048]{1,0:T(8,128)S(1)} fusion(f32[512,2048]{0,1:T(8,128)S(1)} %bitcast.120, s32[512]{0:T(512)S(1)} %fusion.207), kind=kOutput, calls=%fused_computation.252 | convolution fusion | flops 1610678272 | bytes 5244928 | tf_op jit(solution)/shard_map/dot_general | solution.py:130
  134.1 14.6 %fusion = f32[16,128,128]{2,1,0:T(8,128)S(1)} fusion(f32[128,16,128]{2,0,1:T(8,128)S(1)} %bitcast.121, f32[128,16,128]{2,0,1:T(8,128)S(1)} %bitcast.122, f32[16,128]{1,0:T(8,128)} %bitcast.140, f32[16,128]{1,0:T(8,128)} %bitcast.141, f32[16,128]{1,0:T(8,128)} %bitcast.143, f32[16,128]{1,0:T(8,128)} %bitcast.144, f32[16,128]{1,0:T(8,128)} %bitcast.145, ...), kind=kOutput, calls=%fused_computation.5 | convolution fusion | flops 837812224 | bytes 4415488 | tf_op jit(solution)/shard_map/rgw,gwc->rgc/dot_general | solution.py:56
  148.8 1.3 copy.41
  150.1 12.8 %reduce-scatter.2.cloned.1.call-done = f32[64,2048]{1,0:T(8,128)} async-done(((f32[128,2048]{1,0:T(8,128)}), f32[64,2048]{1,0:T(8,128)}) %reduce-scatter.2.cloned.1.call-update) | async-done | bytes 524304 | tf_op jit(solution)/shard_map/reduce_scatter | solution.py:133
  162.9 1.9 %divide_bitcast_fusion = f32[1,64,2048]{2,1,0:T(8,128)} fusion(f32[64,2048]{1,0:T(8,128)} %reduce-scatter.2.cloned.1.call-done, f32[64]{0:T(128)S(1)} %convert_bitcast_fusion), kind=kLoop, calls=%fused_computation.247 | loop fusion | flops 131072 | bytes 1048832 | tf_op jit(solution)/shard_map/broadcast_in_dim | solution.py:136
  (242 shorter events, 19.0 us)
Async XLA Ops:
  6.5 17.9 %copy-start = (bf16[256,2048]{1,0:T(8,128)(2,1)S(1)}, bf16[256,2048]{1,0:T(8,128)(2,1)}, u32[]{:S(2)}) copy-start(bf16[256,2048]{1,0:T(8,128)(2,1)} %param.8) | copy-start | bytes 3145732
  15.7 25.0 %all-to-all-start = ((s32[16,1,32]{2,1,0:T(1,128)}), s32[16,1,32]{2,1,0:T(1,128)S(1)}, u32[]{:S(2)}, u32[]{:S(2)}) async-start(s32[16,1,32]{2,1,0:T(1,128)} %bitcast.36), calls=%async_computation | async-start | bytes 16384 | tf_op jit(solution)/shard_map/all_to_all | solution.py:120
  40.7 13.3 %copy-start.2 = (f32[31,2048]{1,0:T(8,128)S(1)}, f32[31,2048]{1,0:T(8,128)}, u32[]{:S(2)}) copy-start(f32[31,2048]{1,0:T(8,128)} %param.14) | copy-start | bytes 761860
  40.7 14.7 %copy-start.3 = (bf16[1,4,8,2048]{3,2,1,0:T(8,128)(2,1)S(1)}, bf16[1,4,8,2048]{3,2,1,0:T(8,128)(2,1)}, u32[]{:S(2)}) copy-start(bf16[1,4,8,2048]{3,2,1,0:T(8,128)(2,1)} %param.12) | copy-start | bytes 393220
  40.7 49.8 %all-to-all-start.1 = ((bf16[16,32,2048]{2,1,0:T(8,128)(2,1)}), bf16[16,32,2048]{2,1,0:T(8,128)(2,1)S(1)}, u32[]{:S(2)}, u32[]{:S(2)}) async-start(bf16[16,32,2048]{2,1,0:T(8,128)(2,1)} %select_select_fusion), calls=%async_computation.1 | async-start | bytes 4194304 | tf_op jit(solution)/shard_map/all_to_all | solution.py:113
  47.7 115.2 %reduce-scatter.2.cloned.1.call-start = ((), (), s32[]{:S(2)}) async-start(), calls=%async_computation.3 | async-start | bytes 1572864 | tf_op jit(solution)/shard_map/reduce_scatter | solution.py:133
  102.1 7.5 %copy-start.61 = (s32[16,128]{1,0:T(8,128)S(1)}, s32[16,128]{1,0:T(8,128)}, u32[]{:S(2)}) copy-start(s32[16,128]{1,0:T(8,128)} %get-tuple-element.96) | copy-start | bytes 24580
  102.1 7.5 %copy-start.62 = (s32[16,128]{1,0:T(8,128)S(1)}, s32[16,128]{1,0:T(8,128)}, u32[]{:S(2)}) copy-start(s32[16,128]{1,0:T(8,128)} %get-tuple-element.97) | copy-start | bytes 24580
  102.1 7.5 %copy-start.63 = (s32[16,128]{1,0:T(8,128)S(1)}, s32[16,128]{1,0:T(8,128)}, u32[]{:S(2)}) copy-start(s32[16,128]{1,0:T(8,128)} %get-tuple-element.98) | copy-start | bytes 24580
  102.2 7.5 %copy-start.64 = (s32[16,128]{1,0:T(8,128)S(1)}, s32[16,128]{1,0:T(8,128)}, u32[]{:S(2)}) copy-start(s32[16,128]{1,0:T(8,128)} %get-tuple-element.99) | copy-start | bytes 24580
  102.2 7.5 %copy-start.65 = (s32[16,128]{1,0:T(8,128)S(1)}, s32[16,128]{1,0:T(8,128)}, u32[]{:S(2)}) copy-start(s32[16,128]{1,0:T(8,128)} %get-tuple-element.100) | copy-start | bytes 24580
  102.2 7.5 %copy-start.66 = (s32[16,128]{1,0:T(8,128)S(1)}, s32[16,128]{1,0:T(8,128)}, u32[]{:S(2)}) copy-start(s32[16,128]{1,0:T(8,128)} %get-tuple-element.101) | copy-start | bytes 24580
  102.2 7.5 %copy-start.67 = (s32[16,128]{1,0:T(8,128)S(1)}, s32[16,128]{1,0:T(8,128)}, u32[]{:S(2)}) copy-start(s32[16,128]{1,0:T(8,128)} %get-tuple-element.102) | copy-start | bytes 24580
  102.2 7.5 %copy-start.68 = (s32[16,128]{1,0:T(8,128)S(1)}, s32[16,128]{1,0:T(8,128)}, u32[]{:S(2)}) copy-start(s32[16,128]{1,0:T(8,128)} %get-tuple-element.103) | copy-start | bytes 24580
  102.2 7.5 %copy-start.77 = (f32[1,1,1,2048]{3,2,1,0:T(1,128)S(1)}, f32[1,1,1,2048]{3,2,1,0:T(1,128)}, u32[]{:S(2)}) copy-start(f32[1,1,1,2048]{3,2,1,0:T(1,128)} %get-tuple-element.67) | copy-start | bytes 24580
  109.8 7.5 %copy-start.53 = (s32[16,128]{1,0:T(8,128)S(1)}, s32[16,128]{1,0:T(8,128)}, u32[]{:S(2)}) copy-start(s32[16,128]{1,0:T(8,128)} %get-tuple-element.104) | copy-start | bytes 24580
  109.8 7.5 %copy-start.54 = (s32[16,128]{1,0:T(8,128)S(1)}, s32[16,128]{1,0:T(8,128)}, u32[]{:S(2)}) copy-start(s32[16,128]{1,0:T(8,128)} %get-tuple-element.105) | copy-start | bytes 24580
  109.8 7.5 %copy-start.55 = (s32[16,128]{1,0:T(8,128)S(1)}, s32[16,128]{1,0:T(8,128)}, u32[]{:S(2)}) copy-start(s32[16,128]{1,0:T(8,128)} %get-tuple-element.106) | copy-start | bytes 24580
  109.8 7.5 %copy-start.56 = (s32[16,128]{1,0:T(8,128)S(1)}, s32[16,128]{1,0:T(8,128)}, u32[]{:S(2)}) copy-start(s32[16,128]{1,0:T(8,128)} %get-tuple-element.107) | copy-start | bytes 24580
  109.8 7.5 %copy-start.57 = (s32[16,128]{1,0:T(8,128)S(1)}, s32[16,128]{1,0:T(8,128)}, u32[]{:S(2)}) copy-start(s32[16,128]{1,0:T(8,128)} %get-tuple-element.108) | copy-start | bytes 24580
  109.8 7.5 %copy-start.58 = (s32[16,128]{1,0:T(8,128)S(1)}, s32[16,128]{1,0:T(8,128)}, u32[]{:S(2)}) copy-start(s32[16,128]{1,0:T(8,128)} %get-tuple-element.109) | copy-start | bytes 24580
  117.4 7.6 %copy-start.45 = (s32[16,128]{1,0:T(8,128)S(1)}, s32[16,128]{1,0:T(8,128)}, u32[]{:S(2)}) copy-start(s32[16,128]{1,0:T(8,128)} %get-tuple-element.80) | copy-start | bytes 24580
  117.4 7.6 %copy-start.46 = (s32[16,128]{1,0:T(8,128)S(1)}, s32[16,128]{1,0:T(8,128)}, u32[]{:S(2)}) copy-start(s32[16,128]{1,0:T(8,128)} %get-tuple-element.81) | copy-start | bytes 24580
  117.4 7.6 %copy-start.47 = (s32[16,128]{1,0:T(8,128)S(1)}, s32[16,128]{1,0:T(8,128)}, u32[]{:S(2)}) copy-start(s32[16,128]{1,0:T(8,128)} %get-tuple-element.82) | copy-start | bytes 24580
  117.4 7.6 %copy-start.48 = (s32[16,128]{1,0:T(8,128)S(1)}, s32[16,128]{1,0:T(8,128)}, u32[]{:S(2)}) copy-start(s32[16,128]{1,0:T(8,128)} %get-tuple-element.83) | copy-start | bytes 24580
  117.4 7.6 %copy-start.49 = (s32[16,128]{1,0:T(8,128)S(1)}, s32[16,128]{1,0:T(8,128)}, u32[]{:S(2)}) copy-start(s32[16,128]{1,0:T(8,128)} %get-tuple-element.84) | copy-start | bytes 24580
  117.4 7.6 %copy-start.50 = (s32[16,128]{1,0:T(8,128)S(1)}, s32[16,128]{1,0:T(8,128)}, u32[]{:S(2)}) copy-start(s32[16,128]{1,0:T(8,128)} %get-tuple-element.85) | copy-start | bytes 24580
  117.4 7.6 %copy-start.51 = (s32[16,128]{1,0:T(8,128)S(1)}, s32[16,128]{1,0:T(8,128)}, u32[]{:S(2)}) copy-start(s32[16,128]{1,0:T(8,128)} %get-tuple-element.86) | copy-start | bytes 24580
  117.4 7.6 %copy-start.52 = (s32[16,128]{1,0:T(8,128)S(1)}, s32[16,128]{1,0:T(8,128)}, u32[]{:S(2)}) copy-start(s32[16,128]{1,0:T(8,128)} %get-tuple-element.87) | copy-start | bytes 24580
  117.5 7.6 %copy-start.78 = (pred[512]{0:T(512)(128)(4,1)S(1)}, pred[512]{0:T(512)(128)(4,1)}, u32[]{:S(2)}) copy-start(pred[512]{0:T(512)(128)(4,1)} %get-tuple-element.112) | copy-start | bytes 1540
  117.5 7.6 %copy-start.79 = (pred[512]{0:T(512)(128)(4,1)S(1)}, pred[512]{0:T(512)(128)(4,1)}, u32[]{:S(2)}) copy-start(pred[512]{0:T(512)(128)(4,1)} %get-tuple-element.113) | copy-start | bytes 1540
  117.5 7.6 %copy-start.80 = (pred[512]{0:T(512)(128)(4,1)S(1)}, pred[512]{0:T(512)(128)(4,1)}, u32[]{:S(2)}) copy-start(pred[512]{0:T(512)(128)(4,1)} %get-tuple-element.114) | copy-start | bytes 1540
  (53 other events, 68.1 us)
Sparse Core Ops, SparseCore 0:
  150.2 12.6 reduce-scatter.1
where the time goes:
time: 172 us
  waiting for transfers between devices  45.3 us (26%)
  matrix products  44.1 us (26%)
  other arithmetic  27.5 us (16%)
  local copies, waits for them, and re-layouts  24.4 us (14%)
  starting transfers between devices  15.6 us (9%)
  between operations  14.7 us (9%)
    all_to_all x1, waiting for transfers between devices, body(): lax.all_to_all(rows_out.reshape(line_count, capacity, length), 'line', sp...  32.5 us
    dot_general x4, matrix products, moveout(): jnp.einsum('sgw,gwc->sgc', window_rows, matrix, preferred_element_type=jn...  27 us
    dot_general x1, matrix products, apply_filter(): jnp.einsum('rgw,gwc->rgc', windows(stacked, 64), matrix, precision=lax.Pr...  14.6 us
    reduce_scatter x1, waiting for transfers between devices, body(): lax.psum_scatter(apply_filter(stacked, filter_weights), 'tile', scatter_d...  12.8 us
    eq x16, other arithmetic, bandpass_matrix(): position == column + 64 + tap_index - half  12.2 us
    all_to_all x1, starting transfers between devices, body(): lax.all_to_all(meta_out.reshape(line_count, capacity), 'line', split_axis...  8.31 us
    all_to_all x1, starting transfers between devices, body(): lax.all_to_all(rows_out.reshape(line_count, capacity, length), 'line', sp...  7.04 us
    slice x2, local copies, waits for them, and re-layouts, windows(): second = padded[:, 128:length + 128].reshape(rows_count, groups, 128)  5.42 us
  transfers between devices with their start and end apart: 3, of which 2 were waited for; matrix products, arithmetic and copies ran while one was open for 15% of the time, Pallas kernels for 0%

commit v1 on v0

v1 whole, which is shorter than its diff:
```python
import functools

import jax
import jax.numpy as jnp
from jax import lax
from jax.experimental import pallas as pl
from jax.experimental.pallas import tpu as pltpu
from jax.sharding import PartitionSpec as P

LANES = 128
CHUNK = 128
MESH = pl.DeviceIdType.MESH


def iota(shape, dim):
    return lax.broadcasted_iota(jnp.int32, shape, dim)


def to_column(row):
    n = row.shape[1]
    wide = jnp.broadcast_to(row, (n, n))
    return jnp.sum(jnp.where(iota((n, n), 0) == iota((n, n), 1), wide, 0.0), 1, keepdims=True)


def dot(a, b):
    return jnp.dot(a, b, preferred_element_type=jnp.float32)


def split(value):
    high = value.astype(jnp.bfloat16)
    low = (value - high.astype(jnp.float32)).astype(jnp.bfloat16)
    return high, low


def kernel(
    n_line, n_tile, cap, noff, taps,
    traces, line_ref, bin_ref, block_ref, coef, shift, band, fold_ref,
    out,
    packed, landed, total, halves, nmo, bp_high, bp_low, shifted,
    send_sem, recv_sem,
):
    n = n_line * n_tile
    me = lax.axis_index("line") * n_tile + lax.axis_index("tile")
    trace_count, length = traces.shape
    share = out.shape[0]
    ids = noff * share
    groups = length // LANES
    per_chunk = CHUNK // cap
    chunks = n // per_chunk
    filter_taps = band.shape[0]
    half = (filter_taps - 1) // 2

    def place(index):
        return (index // n_tile, index % n_tile)

    barrier = pltpu.get_barrier_semaphore()

    @pl.loop(1, n)
    def _(k):
        pl.semaphore_signal(barrier, inc=1, device_id=place((me + k) % n), device_id_type=MESH)

    bins = bin_ref[...]
    tile = jnp.zeros_like(bins)
    for t in range(1, n_tile):
        tile = tile + jnp.where(bins >= t * share, 1, 0)
    offset = line_ref[...] * n_tile + tile - me
    offset = jnp.where(offset < 0, offset + n, offset).astype(jnp.float32)
    same = (to_column(offset) == offset) & (
        iota((trace_count, trace_count), 0) < iota((trace_count, trace_count), 1)
    )
    rank = jnp.sum(jnp.where(same, 1.0, 0.0), 0, keepdims=True)
    slot = offset * cap + rank
    block = trace_count // block_ref.shape[0]
    spot = iota((1, trace_count), 1)
    trace_class = jnp.zeros((1, trace_count), jnp.int32)
    for b in range(block_ref.shape[0]):
        inside = (spot >= b * block) & (spot < (b + 1) * block)
        trace_class = jnp.where(inside, block_ref[b], trace_class)
    ident = (trace_class * share + bins - tile * share).astype(jnp.float32)
    ident = jnp.broadcast_to(to_column(ident), (trace_count, LANES)).astype(jnp.bfloat16)

    def pack(chunk):
        base = chunk * CHUNK
        rows = (iota((CHUNK, trace_count), 0) + base).astype(jnp.float32)
        pick = jnp.where(rows == slot, 1.0, 0.0).astype(jnp.bfloat16)
        width = 512

        @pl.loop(0, length // width)
        def _(j):
            cols = pl.ds(pl.multiple_of(j * width, width), width)
            packed[pl.ds(base, CHUNK), cols] = dot(pick, traces[:, cols]).astype(jnp.bfloat16)

        packed[pl.ds(base, CHUNK), pl.ds(length, LANES)] = dot(pick, ident).astype(jnp.bfloat16)

    def copy(k):
        rows = pl.ds(pl.multiple_of(k * cap, cap), cap)
        return pltpu.make_async_remote_copy(
            src_ref=packed.at[rows],
            dst_ref=landed.at[rows],
            send_sem=send_sem.at[k],
            recv_sem=recv_sem.at[k],
            device_id=place((me + k) % n),
            device_id_type=MESH,
        )

    order = sorted(range(chunks), key=lambda c: abs(c * per_chunk - n // 2))
    for number, chunk in enumerate(order):
        pack(chunk)
        if number == 0:
            pl.semaphore_wait(barrier, n - 1)

        @pl.loop(max(chunk * per_chunk, 1), (chunk + 1) * per_chunk)
        def _(k):
            copy(k).start()

        if chunk == 0:
            landed[0:cap] = packed[0:cap]

    position = iota((2 * LANES, LANES), 0) - iota((2 * LANES, LANES), 1)

    @pl.loop(0, groups)
    def _(g):
        cols = pl.ds(pl.multiple_of(g * LANES, LANES), LANES)
        for c in range(noff):
            place_rel = position - shift[c : c + 1, cols]
            weights = coef[c * taps : (c + 1) * taps, cols].astype(jnp.float32)
            matrix = jnp.zeros((2 * LANES, LANES), jnp.float32)
            for b in range(taps):
                matrix = jnp.where(place_rel == b, weights[b : b + 1], matrix)
            nmo[g * noff + c] = matrix.astype(jnp.bfloat16)
        matrix = jnp.zeros((2 * LANES, LANES), jnp.float32)
        for b in range(filter_taps):
            matrix = jnp.where(position == LANES // 2 + b - half, band[b : b + 1, cols], matrix)
        high, low = split(matrix)
        bp_high[g] = high
        bp_low[g] = low

    for c in range(noff):
        halves[c, :, pl.ds(length, LANES)] = jnp.zeros((2 * share, LANES), jnp.bfloat16)
    scale = 1.0 / to_column(fold_ref[...].astype(jnp.float32))

    for number, chunk in enumerate(order):

        @pl.loop(max(chunk * per_chunk, 1), (chunk + 1) * per_chunk)
        def _(k):
            copy(k).wait_recv()

        base = chunk * CHUNK
        names = landed[pl.ds(base, CHUNK), pl.ds(length, LANES)].astype(jnp.float32)
        names = jnp.transpose(names)[0:1, :]
        chosen = jnp.where(iota((ids, CHUNK), 0).astype(jnp.float32) == names, 1.0, 0.0)
        chosen = chosen.astype(jnp.bfloat16)
        width = 256

        @pl.loop(0, length // width)
        def _(j):
            cols = pl.ds(pl.multiple_of(j * width, width), width)
            part = dot(chosen, landed[pl.ds(base, CHUNK), cols])
            if number > 0:
                part = part + total[:, cols]
            if number < chunks - 1:
                total[:, cols] = part
            else:
                high, low = split(part)
                for c in range(noff):
                    halves[c, 0:share, cols] = high[c * share : (c + 1) * share]
                    halves[c, share : 2 * share, cols] = low[c * share : (c + 1) * share]

    left = iota((share, LANES), 1) < LANES // 2

    def store_shifted(g, value):
        high, low = split(value)
        cols = pl.ds(g * LANES, LANES)
        shifted[0:share, cols] = high
        shifted[share : 2 * share, cols] = low

    def bandpass(g):
        window = shifted[:, pl.ds(g * LANES, 2 * LANES)]
        first = dot(window, bp_high[g])
        second = dot(window[0:share], bp_low[g])
        out[:, pl.ds(g * LANES, LANES)] = (first[0:share] + first[share:] + second) * scale

    before = jnp.zeros((share, LANES), jnp.float32)
    for g in range(groups):
        acc = dot(halves[0, :, pl.ds(g * LANES, 2 * LANES)], nmo[g * noff])
        for c in range(1, noff):
            acc = acc + dot(halves[c, :, pl.ds(g * LANES, 2 * LANES)], nmo[g * noff + c])
        turned = pltpu.roll(acc[0:share] + acc[share:], LANES // 2, 1)
        store_shifted(g, jnp.where(left, before, turned))
        before = turned
        if g >= 1:
            bandpass(g - 1)
    store_shifted(groups, jnp.where(left, before, 0.0))
    bandpass(groups - 1)

    @pl.loop(1, n)
    def _(k):
        copy(k).wait_send()


def body(traces, trace_line, trace_bin, block_offset, nmo_coef, band_shift, bandpass, fold):
    n_line = lax.axis_size("line")
    n_tile = lax.axis_size("tile")
    n = n_line * n_tile
    trace_count, length = traces.shape
    share = fold.shape[1]
    noff, taps = nmo_coef.shape[1:3]
    groups = length // LANES
    cap = -(-(2 * trace_count // n) // 16) * 16
    rows = n * cap
    vmem = pl.BlockSpec(memory_space=pltpu.VMEM)
    result = pl.pallas_call(
        functools.partial(kernel, n_line, n_tile, cap, noff, taps),
        out_shape=jax.ShapeDtypeStruct((share, length), jnp.float32),
        in_specs=[vmem, vmem, vmem, pl.BlockSpec(memory_space=pltpu.SMEM), vmem, vmem, vmem, vmem],
        out_specs=vmem,
        scratch_shapes=[
            pltpu.VMEM((rows, length + LANES), jnp.bfloat16),
            pltpu.VMEM((rows, length + LANES), jnp.bfloat16),
            pltpu.VMEM((noff * share, length), jnp.float32),
            pltpu.VMEM((noff, 2 * share, length + LANES), jnp.bfloat16),
            pltpu.VMEM((groups * noff, 2 * LANES, LANES), jnp.bfloat16),
            pltpu.VMEM((groups, 2 * LANES, LANES), jnp.bfloat16),
            pltpu.VMEM((groups, 2 * LANES, LANES), jnp.bfloat16),
            pltpu.VMEM((2 * share, length + LANES), jnp.bfloat16),
            pltpu.SemaphoreType.DMA((n,)),
            pltpu.SemaphoreType.DMA((n,)),
        ],
        compiler_params=pltpu.CompilerParams(
            collective_id=0, has_side_effects=True, vmem_limit_bytes=50 * 1024 * 1024
        ),
        name="route_and_stack",
    )(
        traces,
        trace_line.reshape(1, -1),
        trace_bin.reshape(1, -1),
        block_offset,
        nmo_coef.reshape(noff * taps, length),
        band_shift.reshape(noff, length),
        bandpass,
        fold,
    )
    return result[None]


def solution(mesh):
    placed = (
        P(("line", "tile"), None),
        P(("line", "tile")),
        P(("line", "tile")),
        P(("line", "tile")),
        P("line", None, None, None),
        P("line", None, None),
        P(),
        P("line", "tile"),
    )
    return jax.shard_map(
        body, mesh=mesh, in_specs=placed, out_specs=P("line", "tile", None), check_vma=False
    )
```

time: 172 us -> 71.7 us (0.42)
  the two profiles are of different devices: /device:TPU:0 before, /device:TPU:15 now
where the time goes in v1:
time: 71.7 us; the launch traced here: 71.5 us
  Pallas kernels  66.1 us (92%)
  local copies, waits for them, and re-layouts  5.33 us (7%)
    pallas_call x1, Pallas kernels, body(): pl.pallas_call(functools.partial(kernel, n_line, n_tile, cap, noff, taps)...  66.1 us
    unnamed x17, local copies, waits for them, and re-layouts  5.33 us

profile of v1, /device:TPU:15, one launch (start us, length us, event | category | flops | bytes accessed | tf_op | source)
XLA Modules:
  0.0 71.5 jit_solution(12582771751328381702)
XLA Ops:
  0.0 0.0 copy-start.5
  0.0 0.0 copy-start.7
  0.0 0.0 copy-start.4
  0.0 0.0 copy-start.6
  0.0 0.7 copy-done.5
  0.7 0.0 copy-done.7
  0.7 0.0 copy-done.4
  0.7 0.0 copy-done.6
  0.7 0.0 copy-start
  0.7 1.2 %copy-done = bf16[256,2048]{1,0:T(8,128)(2,1)S(1)} copy-done((bf16[256,2048]{1,0:T(8,128)(2,1)S(1)}, bf16[256,2048]{1,0:T(8,128)(2,1)}, u32[]{:S(2)}) %copy-start) | copy-done | bytes 1048600
  1.9 0.0 copy-start.1
  1.9 0.9 %copy-done.1 = f32[31,2048]{1,0:T(8,128)S(1)} copy-done((f32[31,2048]{1,0:T(8,128)S(1)}, f32[31,2048]{1,0:T(8,128)}, u32[]{:S(2)}) %copy-start.1) | copy-done | bytes 253976
  2.9 0.0 copy-start.2
  2.9 0.9 %copy-done.2 = bf16[1,4,8,2048]{3,2,1,0:T(8,128)(2,1)S(1)} copy-done((bf16[1,4,8,2048]{3,2,1,0:T(8,128)(2,1)S(1)}, bf16[1,4,8,2048]{3,2,1,0:T(8,128)(2,1)}, u32[]{:S(2)}) %copy-start.2) | copy-done | bytes 131096
  3.8 0.0 copy-start.3
  3.8 0.8 %copy-done.3 = s32[1,4,2048]{2,1,0:T(4,128)S(1)} copy-done((s32[1,4,2048]{2,1,0:T(4,128)S(1)}, s32[1,4,2048]{2,1,0:T(4,128)}, u32[]{:S(2)}) %copy-start.3) | copy-done | bytes 32792
  4.6 66.1 %route_and_stack.1 = f32[64,2048]{1,0:T(8,128)S(1)} custom-call(bf16[256,2048]{1,0:T(8,128)(2,1)S(1)} %copy-done, s32[1,256]{1,0:T(1,128)S(1)} %bitcast.8, s32[1,256]{1,0:T(1,128)S(1)} %bitcast.9, s32[2]{0:T(128)S(1)} %copy-done.6, bf16[32,2048]{1,0:T(8,128)(2,1)S(1)} %bitcast.6, s32[4,2048]{1,0:T(4,128)S(1)} %bitcast.7, f32[31,2048]{1,0:T(8,128)S(1)} %copy-done.1, ...), custom_call_target="tpu_custom_call" | custom-call | tf_op jit(solution)/shard_map/route_and_stack/pallas_call | solution.py:212
  70.7 0.8 %copy.10 = f32[1,64,2048]{2,1,0:T(8,128)} copy(f32[1,64,2048]{2,1,0:T(8,128)S(1)} %bitcast.5) | data formatting | bytes 1048576
Async XLA Ops:
  0.0 0.7 copy-start.5
  0.0 0.7 copy-start.7
  0.0 0.7 copy-start.4
  0.0 0.7 copy-start.6
  0.7 1.2 %copy-start = (bf16[256,2048]{1,0:T(8,128)(2,1)S(1)}, bf16[256,2048]{1,0:T(8,128)(2,1)}, u32[]{:S(2)}) copy-start(bf16[256,2048]{1,0:T(8,128)(2,1)} %traces.1) | copy-start | bytes 3145732
  1.9 0.9 %copy-start.1 = (f32[31,2048]{1,0:T(8,128)S(1)}, f32[31,2048]{1,0:T(8,128)}, u32[]{:S(2)}) copy-start(f32[31,2048]{1,0:T(8,128)} %band.1) | copy-start | bytes 761860
  2.9 0.9 %copy-start.2 = (bf16[1,4,8,2048]{3,2,1,0:T(8,128)(2,1)S(1)}, bf16[1,4,8,2048]{3,2,1,0:T(8,128)(2,1)}, u32[]{:S(2)}) copy-start(bf16[1,4,8,2048]{3,2,1,0:T(8,128)(2,1)} %param.12) | copy-start | bytes 393220
  3.8 0.8 %copy-start.3 = (s32[1,4,2048]{2,1,0:T(4,128)S(1)}, s32[1,4,2048]{2,1,0:T(4,128)}, u32[]{:S(2)}) copy-start(s32[1,4,2048]{2,1,0:T(4,128)} %param.13) | copy-start | bytes 98308

commit v2 on v1

v2 whole, which is shorter than its diff:
```python
import functools

import jax
import jax.numpy as jnp
from jax import lax
from jax.experimental import pallas as pl
from jax.experimental.pallas import tpu as pltpu
from jax.sharding import PartitionSpec as P

LANES = 128
CHUNK = 128
PARTS = 2
MESH = pl.DeviceIdType.MESH


def iota(shape, dim):
    return lax.broadcasted_iota(jnp.int32, shape, dim)


def to_column(row):
    n = row.shape[1]
    wide = jnp.broadcast_to(row, (n, n))
    return jnp.sum(jnp.where(iota((n, n), 0) == iota((n, n), 1), wide, 0.0), 1, keepdims=True)


def dot(a, b):
    return jnp.dot(a, b, preferred_element_type=jnp.float32)


def split(value):
    high = value.astype(jnp.bfloat16)
    low = (value - high.astype(jnp.float32)).astype(jnp.bfloat16)
    return high, low


def kernel(
    n_line, n_tile, cap, noff, taps,
    traces_hbm, line_hbm, bin_hbm, block_hbm, coef_hbm, shift_hbm, band_hbm, fold_hbm,
    out,
    traces, line_ref, bin_ref, block_ref, coef, shift, band, fold_ref,
    pick, packed, landed, names_out, names_in, chosen, halves, nmo, bp_high, bp_low, shifted,
    local_sem, part_sem, send_sem, recv_sem, name_send_sem, name_recv_sem,
):
    n = n_line * n_tile
    me = lax.axis_index("line") * n_tile + lax.axis_index("tile")
    trace_count, length = traces.shape
    rows_total = packed.shape[0]
    share = out.shape[0]
    ids = noff * share
    groups = length // LANES
    per_chunk = CHUNK // cap
    chunks = n // per_chunk
    parts = part_sem.shape[0]
    width = length // parts
    filter_taps = band.shape[0]
    half = (filter_taps - 1) // 2

    small = [
        pltpu.make_async_copy(source, target, local_sem.at[index])
        for index, (source, target) in enumerate(
            [
                (line_hbm, line_ref), (bin_hbm, bin_ref), (block_hbm, block_ref),
                (fold_hbm, fold_ref), (shift_hbm, shift), (coef_hbm, coef), (band_hbm, band),
            ]
        )
    ]
    for item in small[:4]:
        item.start()
    pieces = []
    for p in range(parts):
        cols = pl.ds(p * width, width)
        pieces.append(
            pltpu.make_async_copy(traces_hbm.at[:, cols], traces.at[:, cols], part_sem.at[p])
        )
        pieces[p].start()
    for item in small[4:]:
        item.start()

    def place(index):
        return (index // n_tile, index % n_tile)

    barrier = pltpu.get_barrier_semaphore()

    @pl.loop(1, n)
    def _(k):
        pl.semaphore_signal(barrier, inc=1, device_id=place((me + k) % n), device_id_type=MESH)

    for item in small[:4]:
        item.wait()

    bins = bin_ref[...]
    tile = jnp.zeros_like(bins)
    for t in range(1, n_tile):
        tile = tile + jnp.where(bins >= t * share, 1, 0)
    offset = line_ref[...] * n_tile + tile - me
    offset = jnp.where(offset < 0, offset + n, offset).astype(jnp.float32)
    same = (to_column(offset) == offset) & (
        iota((trace_count, trace_count), 0) < iota((trace_count, trace_count), 1)
    )
    rank = jnp.sum(jnp.where(same, 1.0, 0.0), 0, keepdims=True)
    slot = offset * cap + rank

    for chunk in range(chunks):
        rows = (iota((CHUNK, trace_count), 0) + chunk * CHUNK).astype(jnp.float32)
        pick[pl.ds(chunk * CHUNK, CHUNK), :] = jnp.where(rows == slot, 1.0, 0.0).astype(jnp.bfloat16)

    def copy(p, k):
        rows = pl.ds(pl.multiple_of(k * cap, cap), cap)
        cols = pl.ds(p * width, width)
        return pltpu.make_async_remote_copy(
            src_ref=packed.at[rows, cols],
            dst_ref=landed.at[rows, cols],
            send_sem=send_sem.at[p, k],
            recv_sem=recv_sem.at[p, k],
            device_id=place((me + k) % n),
            device_id_type=MESH,
        )

    def name_copy(k):
        return pltpu.make_async_remote_copy(
            src_ref=names_out.at[pl.ds(k, 1)],
            dst_ref=names_in.at[pl.ds(k, 1)],
            send_sem=name_send_sem.at[k],
            recv_sem=name_recv_sem.at[k],
            device_id=place((me + k) % n),
            device_id_type=MESH,
        )

    def far_first(i):
        return 1 + (i + n // 2 - n // 8) % (n - 1)

    for p in range(parts):
        cols = pl.ds(p * width, width)
        pieces[p].wait()

        @pl.loop(0, chunks)
        def _(chunk):
            rows = pl.ds(pl.multiple_of(chunk * CHUNK, CHUNK), CHUNK)
            packed[rows, cols] = dot(pick[rows, :], traces[:, cols]).astype(jnp.bfloat16)

        if p == 0:
            pl.semaphore_wait(barrier, n - 1)

        @pl.loop(0, n - 1)
        def _(i):
            copy(p, far_first(i)).start()

        landed[0:cap, cols] = packed[0:cap, cols]
        if p == 0:
            block = trace_count // block_ref.shape[1]
            spot = iota((1, trace_count), 1)
            trace_class = jnp.zeros((1, trace_count), jnp.int32)
            for b in range(block_ref.shape[1]):
                inside = (spot >= b * block) & (spot < (b + 1) * block)
                value = jnp.broadcast_to(block_ref[:, b : b + 1], (1, trace_count))
                trace_class = jnp.where(inside, value, trace_class)
            ident = (trace_class * share + bins - tile * share).astype(jnp.float32)
            ident = jnp.broadcast_to(to_column(ident), (trace_count, LANES)).astype(jnp.bfloat16)
            for chunk in range(chunks):
                rows = pl.ds(chunk * CHUNK, CHUNK)
                wide = jnp.transpose(dot(pick[rows, :], ident))[0:per_chunk]
                lane = iota((per_chunk, CHUNK), 1)
                first = iota((per_chunk, CHUNK), 0) * cap
                mine = (lane >= first) & (lane < first + cap)
                names_out[pl.ds(chunk * per_chunk, per_chunk), :] = jnp.where(mine, wide, 0.0)

            @pl.loop(0, n - 1)
            def _(i):
                name_copy(far_first(i)).start()

            names_in[0:1] = names_out[0:1]

    for item in small[4:]:
        item.wait()
    position = iota((2 * LANES, LANES), 0) - iota((2 * LANES, LANES), 1)

    @pl.loop(0, groups)
    def _(g):
        cols = pl.ds(pl.multiple_of(g * LANES, LANES), LANES)
        for c in range(noff):
            place_rel = position - shift[c : c + 1, cols]
            weights = coef[c * taps : (c + 1) * taps, cols].astype(jnp.float32)
            matrix = jnp.zeros((2 * LANES, LANES), jnp.float32)
            for b in range(taps):
                matrix = jnp.where(place_rel == b, weights[b : b + 1], matrix)
            nmo[g * noff + c] = matrix.astype(jnp.bfloat16)
        matrix = jnp.zeros((2 * LANES, LANES), jnp.float32)
        for b in range(filter_taps):
            matrix = jnp.where(position == LANES // 2 + b - half, band[b : b + 1, cols], matrix)
        high, low = split(matrix)
        bp_high[g] = high
        bp_low[g] = low

    for c in range(noff):
        halves[c, :, pl.ds(length, LANES)] = jnp.zeros((2 * share, LANES), jnp.bfloat16)
    scale = 1.0 / to_column(fold_ref[...].astype(jnp.float32))

    @pl.loop(1, n)
    def _(k):
        name_copy(k).wait_recv()

    for chunk in range(chunks):
        row = jnp.sum(names_in[pl.ds(chunk * per_chunk, per_chunk), :], 0, keepdims=True)
        hit = iota((ids, CHUNK), 0).astype(jnp.float32) == row
        chosen[:, pl.ds(chunk * CHUNK, CHUNK)] = jnp.where(hit, 1.0, 0.0).astype(jnp.bfloat16)

    left = iota((share, LANES), 1) < LANES // 2

    def store_shifted(g, value):
        high, low = split(value)
        cols = pl.ds(g * LANES, LANES)
        shifted[0:share, cols] = high
        shifted[share : 2 * share, cols] = low

    def bandpass(g):
        window = shifted[:, pl.ds(g * LANES, 2 * LANES)]
        first = dot(window, bp_high[g])
        second = dot(window[0:share], bp_low[g])
        out[:, pl.ds(g * LANES, LANES)] = (first[0:share] + first[share:] + second) * scale

    before = jnp.zeros((share, LANES), jnp.float32)
    done = 0
    for p in range(parts):

        @pl.loop(1, n)
        def _(k):
            copy(p, k).wait_recv()

        step = 2 * LANES
        for j in range(width // step):
            cols = pl.ds(p * width + j * step, step)
            high, low = split(dot(chosen[...], landed[:, cols]))
            for c in range(noff):
                halves[c, 0:share, cols] = high[c * share : (c + 1) * share]
                halves[c, share : 2 * share, cols] = low[c * share : (c + 1) * share]
        ready = groups if p == parts - 1 else (p + 1) * width // LANES - 1
        for g in range(done, ready):
            acc = dot(halves[0, :, pl.ds(g * LANES, 2 * LANES)], nmo[g * noff])
            for c in range(1, noff):
                acc = acc + dot(halves[c, :, pl.ds(g * LANES, 2 * LANES)], nmo[g * noff + c])
            turned = pltpu.roll(acc[0:share] + acc[share:], LANES // 2, 1)
            store_shifted(g, jnp.where(left, before, turned))
            before = turned
            if g >= 1:
                bandpass(g - 1)
        done = ready
    store_shifted(groups, jnp.where(left, before, 0.0))
    bandpass(groups - 1)

    @pl.loop(1, n)
    def _(k):
        name_copy(k).wait_send()
        for p in range(parts):
            copy(p, k).wait_send()


def body(traces, trace_line, trace_bin, block_offset, nmo_coef, band_shift, bandpass, fold):
    n_line = lax.axis_size("line")
    n_tile = lax.axis_size("tile")
    n = n_line * n_tile
    trace_count, length = traces.shape
    share = fold.shape[1]
    noff, taps = nmo_coef.shape[1:3]
    groups = length // LANES
    cap = -(-(2 * trace_count // n) // 16) * 16
    rows = n * cap
    parts = PARTS
    vmem = pl.BlockSpec(memory_space=pltpu.VMEM)
    hbm = pl.BlockSpec(memory_space=pltpu.HBM)
    result = pl.pallas_call(
        functools.partial(kernel, n_line, n_tile, cap, noff, taps),
        out_shape=jax.ShapeDtypeStruct((share, length), jnp.float32),
        in_specs=[hbm] * 8,
        out_specs=vmem,
        scratch_shapes=[
            pltpu.VMEM((trace_count, length), jnp.bfloat16),
            pltpu.VMEM((1, trace_count), jnp.int32),
            pltpu.VMEM((1, trace_count), jnp.int32),
            pltpu.VMEM((1, block_offset.shape[0]), jnp.int32),
            pltpu.VMEM((noff * taps, length), jnp.bfloat16),
            pltpu.VMEM((noff, length), jnp.int32),
            pltpu.VMEM(bandpass.shape, jnp.float32),
            pltpu.VMEM((1, share), jnp.int32),
            pltpu.VMEM((rows, trace_count), jnp.bfloat16),
            pltpu.VMEM((rows, length), jnp.bfloat16),
            pltpu.VMEM((rows, length), jnp.bfloat16),
            pltpu.VMEM((n, LANES), jnp.float32),
            pltpu.VMEM((n, LANES), jnp.float32),
            pltpu.VMEM((noff * share, rows), jnp.bfloat16),
            pltpu.VMEM((noff, 2 * share, length + LANES), jnp.bfloat16),
            pltpu.VMEM((groups * noff, 2 * LANES, LANES), jnp.bfloat16),
            pltpu.VMEM((groups, 2 * LANES, LANES), jnp.bfloat16),
            pltpu.VMEM((groups, 2 * LANES, LANES), jnp.bfloat16),
            pltpu.VMEM((2 * share, length + LANES), jnp.bfloat16),
            pltpu.SemaphoreType.DMA((7,)),
            pltpu.SemaphoreType.DMA((parts,)),
            pltpu.SemaphoreType.DMA((parts, n)),
            pltpu.SemaphoreType.DMA((parts, n)),
            pltpu.SemaphoreType.DMA((n,)),
            pltpu.SemaphoreType.DMA((n,)),
        ],
        compiler_params=pltpu.CompilerParams(
            collective_id=0, has_side_effects=True, vmem_limit_bytes=60 * 1024 * 1024
        ),
        name="route_and_stack",
    )(
        traces,
        trace_line.reshape(1, -1),
        trace_bin.reshape(1, -1),
        block_offset.reshape(1, -1),
        nmo_coef.reshape(noff * taps, length),
        band_shift.reshape(noff, length),
        bandpass,
        fold,
    )
    return result[None]


def solution(mesh):
    placed = (
        P(("line", "tile"), None),
        P(("line", "tile")),
        P(("line", "tile")),
        P(("line", "tile")),
        P("line", None, None, None),
        P("line", None, None),
        P(),
        P("line", "tile"),
    )
    return jax.shard_map(
        body, mesh=mesh, in_specs=placed, out_specs=P("line", "tile", None), check_vma=False
    )
```

time: 71.7 us -> 62.6 us (0.87)
  the two profiles are of different devices: /device:TPU:15 before, /device:TPU:0 now
where the time goes in v2:
time: 62.6 us; the launch traced here: 62.5 us
  Pallas kernels  60.6 us (97%)
  local copies, waits for them, and re-layouts  1.87 us (3%)
    pallas_call x1, Pallas kernels, body(): pl.pallas_call(functools.partial(kernel, n_line, n_tile, cap, noff, taps)...  60.6 us
    unnamed x1, local copies, waits for them, and re-layouts  1.87 us

profile of v2, /device:TPU:0, one launch (start us, length us, event | category | flops | bytes accessed | tf_op | source)
XLA Modules:
  0.0 62.5 jit_solution(13069503751988119179)
XLA Ops:
  0.0 60.6 %route_and_stack.1 = f32[64,2048]{1,0:T(8,128)} custom-call(bf16[256,2048]{1,0:T(8,128)(2,1)} %traces_hbm.1, s32[1,256]{1,0:T(1,128)} %bitcast.9, s32[1,256]{1,0:T(1,128)} %bitcast.10, s32[1,2]{1,0:T(1,128)} %bitcast.11, bf16[32,2048]{1,0:T(8,128)(2,1)} %bitcast.7, s32[4,2048]{1,0:T(4,128)} %bitcast.8, f32[31,2048]{1,0:T(8,128)} %band_hbm.1, s32[1,64]{1,0:T(1,128)} %fold_hbm.1), custom_call_target="tpu_custom_call" | custom-call | tf_op jit(solution)/shard_map/route_and_stack/pallas_call | solution.py:270
  60.6 1.9 %copy.10 = f32[1,64,2048]{2,1,0:T(8,128)} copy(f32[1,64,2048]{2,1,0:T(8,128)} %bitcast.6) | data formatting | bytes 1048576

commit v3 on v2

--- a/solution.py
+++ b/solution.py
@@ -9,7 +9,7 @@
 
 LANES = 128
 CHUNK = 128
-PARTS = 2
+PARTS = 4
 MESH = pl.DeviceIdType.MESH
 
 
@@ -39,12 +39,16 @@
     out,
     traces, line_ref, bin_ref, block_ref, coef, shift, band, fold_ref,
     pick, packed, landed, names_out, names_in, chosen, halves, nmo, bp_high, bp_low, shifted,
+    coef_in, shift_in, sums_out, sums_in,
     local_sem, part_sem, send_sem, recv_sem, name_send_sem, name_recv_sem,
+    far_send_sem, far_recv_sem,
 ):
     n = n_line * n_tile
     me = lax.axis_index("line") * n_tile + lax.axis_index("tile")
+    m = n // 2
+    my_half = me // m
+    spot_in_half = me % m
     trace_count, length = traces.shape
-    rows_total = packed.shape[0]
     share = out.shape[0]
     ids = noff * share
     groups = length // LANES
@@ -81,9 +85,16 @@
 
     barrier = pltpu.get_barrier_semaphore()
 
-    @pl.loop(1, n)
+    mirror = place((me + m) % n)
+
+    def peer(k):
+        return place(my_half * m + (spot_in_half + k) % m)
+
+    @pl.loop(1, m)
     def _(k):
-        pl.semaphore_signal(barrier, inc=1, device_id=place((me + k) % n), device_id_type=MESH)
+        pl.semaphore_signal(barrier, inc=1, device_id=peer(k), device_id_type=MESH)
+
+    pl.semaphore_signal(barrier, inc=1, device_id=mirror, device_id_type=MESH)
 
     for item in small[:4]:
         item.wait()
@@ -92,8 +103,11 @@
     tile = jnp.zeros_like(bins)
     for t in range(1, n_tile):
         tile = tile + jnp.where(bins >= t * share, 1, 0)
-    offset = line_ref[...] * n_tile + tile - me
-    offset = jnp.where(offset < 0, offset + n, offset).astype(jnp.float32)
+    owner = line_ref[...] * n_tile + tile
+    owner_half = jnp.where(owner >= m, 1, 0)
+    offset = owner - owner_half * m - spot_in_half
+    offset = jnp.where(offset < 0, offset + m, offset)
+    offset = jnp.where(owner_half == my_half, offset + m, offset).astype(jnp.float32)
     same = (to_column(offset) == offset) & (
         iota((trace_count, trace_count), 0) < iota((trace_count, trace_count), 1)
     )
@@ -104,48 +118,76 @@
         rows = (iota((CHUNK, trace_count), 0) + chunk * CHUNK).astype(jnp.float32)
         pick[pl.ds(chunk * CHUNK, CHUNK), :] = jnp.where(rows == slot, 1.0, 0.0).astype(jnp.bfloat16)
 
-    def copy(p, k):
-        rows = pl.ds(pl.multiple_of(k * cap, cap), cap)
+    def copy(p, side, k):
+        rows = pl.ds(pl.multiple_of((side * m + k) * cap, cap), cap)
         cols = pl.ds(p * width, width)
         return pltpu.make_async_remote_copy(
             src_ref=packed.at[rows, cols],
             dst_ref=landed.at[rows, cols],
-            send_sem=send_sem.at[p, k],
-            recv_sem=recv_sem.at[p, k],
-            device_id=place((me + k) % n),
+            send_sem=send_sem.at[p, side * m + k],
+            recv_sem=recv_sem.at[p, side * m + k],
+            device_id=peer(k),
             device_id_type=MESH,
         )
 
-    def name_copy(k):
+    def name_copy(side, k):
+        index = side * m + k
         return pltpu.make_async_remote_copy(
-            src_ref=names_out.at[pl.ds(k, 1)],
-            dst_ref=names_in.at[pl.ds(k, 1)],
-            send_sem=name_send_sem.at[k],
-            recv_sem=name_recv_sem.at[k],
-            device_id=place((me + k) % n),
+            src_ref=names_out.at[pl.ds(index, 1)],
+            dst_ref=names_in.at[pl.ds(index, 1)],
+            send_sem=name_send_sem.at[index],
+            recv_sem=name_recv_sem.at[index],
+            device_id=peer(k),
             device_id_type=MESH,
         )
 
-    def far_first(i):
-        return 1 + (i + n // 2 - n // 8) % (n - 1)
-
-    for p in range(parts):
+    def far_copy(index, source, target):
+        return pltpu.make_async_remote_copy(
+            src_ref=source,
+            dst_ref=target,
+            send_sem=far_send_sem.at[index],
+            recv_sem=far_recv_sem.at[index],
+            device_id=mirror,
+            device_id_type=MESH,
+        )
+
+    far_weights = [far_copy(parts, shift, shift_in), far_copy(parts + 1, coef, coef_in)]
+
+    ends = [(p + 1) * width // LANES - 1 for p in range(parts - 1)] + [groups]
+    starts = [0] + ends[:-1]
+    far_sums = []
+    for p in range(parts):
+        cols = pl.ds(starts[p] * LANES, (ends[p] - starts[p]) * LANES)
+        far_sums.append(far_copy(p, sums_out.at[:, cols], sums_in.at[:, cols]))
+
+    def turn(i):
+        return 1 + (i + m // 2 - 1) % (m - 1)
+
+    def start_part(side, p):
         cols = pl.ds(p * width, width)
+
+        @pl.loop(0, chunks // 2)
+        def _(chunk):
+            rows = pl.ds(pl.multiple_of((side * (chunks // 2) + chunk) * CHUNK, CHUNK), CHUNK)
+            packed[rows, cols] = dot(pick[rows, :], traces[:, cols]).astype(jnp.bfloat16)
+
+        if side == 0 and p == 0:
+            pl.semaphore_wait(barrier, m)
+            for item in small[4:6]:
+                item.wait()
+            for item in far_weights:
+                item.start()
+
+        @pl.loop(0, m - 1)
+        def _(i):
+            copy(p, side, turn(i)).start()
+
+        rows = pl.ds(side * m * cap, cap)
+        landed[rows, cols] = packed[rows, cols]
+
+    for p in range(parts):
         pieces[p].wait()
-
-        @pl.loop(0, chunks)
-        def _(chunk):
-            rows = pl.ds(pl.multiple_of(chunk * CHUNK, CHUNK), CHUNK)
-            packed[rows, cols] = dot(pick[rows, :], traces[:, cols]).astype(jnp.bfloat16)
-
-        if p == 0:
-            pl.semaphore_wait(barrier, n - 1)
-
-        @pl.loop(0, n - 1)
-        def _(i):
-            copy(p, far_first(i)).start()
-
-        landed[0:cap, cols] = packed[0:cap, cols]
+        start_part(0, p)
         if p == 0:
             block = trace_count // block_ref.shape[1]
             spot = iota((1, trace_count), 1)
@@ -164,26 +206,81 @@
                 mine = (lane >= first) & (lane < first + cap)
                 names_out[pl.ds(chunk * per_chunk, per_chunk), :] = jnp.where(mine, wide, 0.0)
 
-            @pl.loop(0, n - 1)
+            @pl.loop(0, m - 1)
             def _(i):
-                name_copy(far_first(i)).start()
+                name_copy(0, turn(i)).start()
+                name_copy(1, turn(i)).start()
 
             names_in[0:1] = names_out[0:1]
-
-    for item in small[4:]:
-        item.wait()
+            names_in[m : m + 1] = names_out[m : m + 1]
+
+    for p in range(parts):
+        start_part(1, p)
+
     position = iota((2 * LANES, LANES), 0) - iota((2 * LANES, LANES), 1)
+
+    def moveout_matrices(side, weights_ref, shifts_ref):
+        @pl.loop(0, groups)
+        def _(g):
+            cols = pl.ds(pl.multiple_of(g * LANES, LANES), LANES)
+            for c in range(noff):
+                place_rel = position - shifts_ref[c : c + 1, cols]
+                weights = weights_ref[c * taps : (c + 1) * taps, cols].astype(jnp.float32)
+                matrix = jnp.zeros((2 * LANES, LANES), jnp.float32)
+                for b in range(taps):
+                    matrix = jnp.where(place_rel == b, weights[b : b + 1], matrix)
+                nmo[side, g * noff + c] = matrix.astype(jnp.bfloat16)
+
+    for item in far_weights:
+        item.wait_recv()
+    moveout_matrices(0, coef_in, shift_in)
+
+    for c in range(noff):
+        halves[c, :, pl.ds(length, LANES)] = jnp.zeros((2 * share, LANES), jnp.bfloat16)
+    scale = 1.0 / to_column(fold_ref[...].astype(jnp.float32))
+
+    @pl.loop(1, m)
+    def _(k):
+        name_copy(0, k).wait_recv()
+        name_copy(1, k).wait_recv()
+
+    for chunk in range(chunks):
+        row = jnp.sum(names_in[pl.ds(chunk * per_chunk, per_chunk), :], 0, keepdims=True)
+        hit = iota((ids, CHUNK), 0).astype(jnp.float32) == row
+        chosen[:, pl.ds(chunk * CHUNK, CHUNK)] = jnp.where(hit, 1.0, 0.0).astype(jnp.bfloat16)
+
+    def sums(side, p):
+        @pl.loop(1, m)
+        def _(k):
+            copy(p, side, k).wait_recv()
+
+        step = 2 * LANES
+        rows = pl.ds(side * m * cap, m * cap)
+        for j in range(width // step):
+            cols = pl.ds(p * width + j * step, step)
+            high, low = split(dot(chosen[:, rows], landed[rows, cols]))
+            for c in range(noff):
+                halves[c, 0:share, cols] = high[c * share : (c + 1) * share]
+                halves[c, share : 2 * share, cols] = low[c * share : (c + 1) * share]
+
+    def moveout(side, g):
+        acc = dot(halves[0, :, pl.ds(g * LANES, 2 * LANES)], nmo[side, g * noff])
+        for c in range(1, noff):
+            acc = acc + dot(halves[c, :, pl.ds(g * LANES, 2 * LANES)], nmo[side, g * noff + c])
+        return acc[0:share] + acc[share:]
+
+    for p in range(parts):
+        sums(0, p)
+        for g in range(starts[p], ends[p]):
+            sums_out[:, pl.ds(g * LANES, LANES)] = moveout(0, g)
+        far_sums[p].start()
+
+    moveout_matrices(1, coef, shift)
+    small[6].wait()
 
     @pl.loop(0, groups)
     def _(g):
         cols = pl.ds(pl.multiple_of(g * LANES, LANES), LANES)
-        for c in range(noff):
-            place_rel = position - shift[c : c + 1, cols]
-            weights = coef[c * taps : (c + 1) * taps, cols].astype(jnp.float32)
-            matrix = jnp.zeros((2 * LANES, LANES), jnp.float32)
-            for b in range(taps):
-                matrix = jnp.where(place_rel == b, weights[b : b + 1], matrix)
-            nmo[g * noff + c] = matrix.astype(jnp.bfloat16)
         matrix = jnp.zeros((2 * LANES, LANES), jnp.float32)
         for b in range(filter_taps):
             matrix = jnp.where(position == LANES // 2 + b - half, band[b : b + 1, cols], matrix)
@@ -191,19 +288,6 @@
         bp_high[g] = high
         bp_low[g] = low
 
-    for c in range(noff):
-        halves[c, :, pl.ds(length, LANES)] = jnp.zeros((2 * share, LANES), jnp.bfloat16)
-    scale = 1.0 / to_column(fold_ref[...].astype(jnp.float32))
-
-    @pl.loop(1, n)
-    def _(k):
-        name_copy(k).wait_recv()
-
-    for chunk in range(chunks):
-        row = jnp.sum(names_in[pl.ds(chunk * per_chunk, per_chunk), :], 0, keepdims=True)
-        hit = iota((ids, CHUNK), 0).astype(jnp.float32) == row
-        chosen[:, pl.ds(chunk * CHUNK, CHUNK)] = jnp.where(hit, 1.0, 0.0).astype(jnp.bfloat16)
-
     left = iota((share, LANES), 1) < LANES // 2
 
     def store_shifted(g, value):
@@ -219,39 +303,29 @@
         out[:, pl.ds(g * LANES, LANES)] = (first[0:share] + first[share:] + second) * scale
 
     before = jnp.zeros((share, LANES), jnp.float32)
-    done = 0
-    for p in range(parts):
-
-        @pl.loop(1, n)
-        def _(k):
-            copy(p, k).wait_recv()
-
-        step = 2 * LANES
-        for j in range(width // step):
-            cols = pl.ds(p * width + j * step, step)
-            high, low = split(dot(chosen[...], landed[:, cols]))
-            for c in range(noff):
-                halves[c, 0:share, cols] = high[c * share : (c + 1) * share]
-                halves[c, share : 2 * share, cols] = low[c * share : (c + 1) * share]
-        ready = groups if p == parts - 1 else (p + 1) * width // LANES - 1
-        for g in range(done, ready):
-            acc = dot(halves[0, :, pl.ds(g * LANES, 2 * LANES)], nmo[g * noff])
-            for c in range(1, noff):
-                acc = acc + dot(halves[c, :, pl.ds(g * LANES, 2 * LANES)], nmo[g * noff + c])
-            turned = pltpu.roll(acc[0:share] + acc[share:], LANES // 2, 1)
+    for p in range(parts):
+        sums(1, p)
+        mine = [moveout(1, g) for g in range(starts[p], ends[p])]
+        far_sums[p].wait_recv()
+        for g in range(starts[p], ends[p]):
+            whole = mine[g - starts[p]] + sums_in[:, pl.ds(g * LANES, LANES)]
+            turned = pltpu.roll(whole, LANES // 2, 1)
             store_shifted(g, jnp.where(left, before, turned))
             before = turned
             if g >= 1:
                 bandpass(g - 1)
-        done = ready
     store_shifted(groups, jnp.where(left, before, 0.0))
     bandpass(groups - 1)
 
-    @pl.loop(1, n)
+    for item in far_weights + far_sums:
+        item.wait_send()
+
+    @pl.loop(1, m)
     def _(k):
-        name_copy(k).wait_send()
-        for p in range(parts):
-            copy(p, k).wait_send()
+        for side in (0, 1):
+            name_copy(side, k).wait_send()
+            for p in range(parts):
+                copy(p, side, k).wait_send()
 
 
 def body(traces, trace_line, trace_bin, block_offset, nmo_coef, band_shift, bandpass, fold):
@@ -288,16 +362,22 @@
             pltpu.VMEM((n, LANES), jnp.float32),
             pltpu.VMEM((noff * share, rows), jnp.bfloat16),
             pltpu.VMEM((noff, 2 * share, length + LANES), jnp.bfloat16),
-            pltpu.VMEM((groups * noff, 2 * LANES, LANES), jnp.bfloat16),
+            pltpu.VMEM((2, groups * noff, 2 * LANES, LANES), jnp.bfloat16),
             pltpu.VMEM((groups, 2 * LANES, LANES), jnp.bfloat16),
             pltpu.VMEM((groups, 2 * LANES, LANES), jnp.bfloat16),
             pltpu.VMEM((2 * share, length + LANES), jnp.bfloat16),
+            pltpu.VMEM((noff * taps, length), jnp.bfloat16),
+            pltpu.VMEM((noff, length), jnp.int32),
+            pltpu.VMEM((share, length), jnp.float32),
+            pltpu.VMEM((share, length), jnp.float32),
             pltpu.SemaphoreType.DMA((7,)),
             pltpu.SemaphoreType.DMA((parts,)),
             pltpu.SemaphoreType.DMA((parts, n)),
             pltpu.SemaphoreType.DMA((parts, n)),
             pltpu.SemaphoreType.DMA((n,)),
             pltpu.SemaphoreType.DMA((n,)),
+            pltpu.SemaphoreType.DMA((parts + 2,)),
+            pltpu.SemaphoreType.DMA((parts + 2,)),
         ],
         compiler_params=pltpu.CompilerParams(
             collective_id=0, has_side_effects=True, vmem_limit_bytes=60 * 1024 * 1024

time: 62.6 us -> 52.4 us (0.84)
  Pallas kernels: 60.6 us -> 50.3 us
    pallas_call x1, Pallas kernels: 60.6 us -> 50.3 us  [body(): pl.pallas_call(functools.partial(kernel, n_line, n_tile, cap, noff, taps)...]
where the time goes in v3:
time: 52.4 us; the launch traced here: 52.2 us
  Pallas kernels  50.3 us (96%)
  local copies, waits for them, and re-layouts  1.87 us (4%)
    pallas_call x1, Pallas kernels, body(): pl.pallas_call(functools.partial(kernel, n_line, n_tile, cap, noff, taps)...  50.3 us
    unnamed x1, local copies, waits for them, and re-layouts  1.87 us

profile of v3, /device:TPU:0, one launch (start us, length us, event | category | flops | bytes accessed | tf_op | source)
XLA Modules:
  0.0 52.2 jit_solution(17417071169957614037)
XLA Ops:
  0.0 50.3 %route_and_stack.1 = f32[64,2048]{1,0:T(8,128)} custom-call(bf16[256,2048]{1,0:T(8,128)(2,1)} %traces_hbm.1, s32[1,256]{1,0:T(1,128)} %bitcast.9, s32[1,256]{1,0:T(1,128)} %bitcast.10, s32[1,2]{1,0:T(1,128)} %bitcast.11, bf16[32,2048]{1,0:T(8,128)(2,1)} %bitcast.7, s32[4,2048]{1,0:T(4,128)} %bitcast.8, f32[31,2048]{1,0:T(8,128)} %band_hbm.1, s32[1,64]{1,0:T(1,128)} %fold_hbm.1), custom_call_target="tpu_custom_call" | custom-call | tf_op jit(solution)/shard_map/route_and_stack/pallas_call | solution.py:344
  50.4 1.9 %copy.10 = f32[1,64,2048]{2,1,0:T(8,128)} copy(f32[1,64,2048]{2,1,0:T(8,128)} %bitcast.6) | data formatting | bytes 1048576

commit v4 on v3

--- a/solution.py
+++ b/solution.py
@@ -9,7 +9,7 @@
 
 LANES = 128
 CHUNK = 128
-PARTS = 4
+PARTS = 2
 MESH = pl.DeviceIdType.MESH
 
 

time: 52.4 us -> 50.8 us (0.969)
  Pallas kernels: 50.3 us -> 48.7 us
    pallas_call x1, Pallas kernels: 50.3 us -> 48.7 us  [body(): pl.pallas_call(functools.partial(kernel, n_line, n_tile, cap, noff, taps)...]
where the time goes in v4:
time: 50.8 us; the launch traced here: 50.6 us
  Pallas kernels  48.7 us (96%)
  local copies, waits for them, and re-layouts  1.87 us (4%)
    pallas_call x1, Pallas kernels, body(): pl.pallas_call(functools.partial(kernel, n_line, n_tile, cap, noff, taps)...  48.7 us
    unnamed x1, local copies, waits for them, and re-layouts  1.87 us

profile of v4, /device:TPU:0, one launch (start us, length us, event | category | flops | bytes accessed | tf_op | source)
XLA Modules:
  0.0 50.6 jit_solution(16930481004361806637)
XLA Ops:
  0.0 48.7 %route_and_stack.1 = f32[64,2048]{1,0:T(8,128)} custom-call(bf16[256,2048]{1,0:T(8,128)(2,1)} %traces_hbm.1, s32[1,256]{1,0:T(1,128)} %bitcast.9, s32[1,256]{1,0:T(1,128)} %bitcast.10, s32[1,2]{1,0:T(1,128)} %bitcast.11, bf16[32,2048]{1,0:T(8,128)(2,1)} %bitcast.7, s32[4,2048]{1,0:T(4,128)} %bitcast.8, f32[31,2048]{1,0:T(8,128)} %band_hbm.1, s32[1,64]{1,0:T(1,128)} %fold_hbm.1), custom_call_target="tpu_custom_call" | custom-call | tf_op jit(solution)/shard_map/route_and_stack/pallas_call | solution.py:344
  48.7 1.9 %copy.10 = f32[1,64,2048]{2,1,0:T(8,128)} copy(f32[1,64,2048]{2,1,0:T(8,128)} %bitcast.6) | data formatting | bytes 1048576
